TPU v7x, 32 devices: a whole 2x2x4 slice. The times are simulated.
32 devices in a mesh: cycle: 2 (over x), gx: 8 (over z, y), gy: 2 (over core).
Axes of the slice: x: 2, y: 2, z: 4, core: 2. Of those that a mesh axis runs over, the one named last changes fastest.
Arguments:
- stored_thermal_state: float32 [128, 64, 1024], P(('cycle', 'gx'), 'gy'), parts along dimension 0, may hold values from 0.2 to 1
- substance_label: int32 [64, 64, 1024], P('gx', 'gy'), may hold values from 0 to 7
- convection_flag: int32 [64, 64, 1024], P('gx', 'gy'), may hold values 0 or 1
- adjoint_source: float32 [128, 64, 1024], P(('cycle', 'gx'), 'gy'), parts along dimension 0, may hold values from -200 to 200
- zero_kelvin_diffusivity: float32 [8], replicated, may hold values from 0.5 to 4
- thermal_coefficient: float32 [8], replicated, may hold values from -0.4 to 0.6
- thermal_storage_rate: float32 [8], replicated, may hold values from 0.3 to 3
Outputs:
- adjoint: float32 [128, 64, 1024], P(('cycle', 'gx'), 'gy'), parts along dimension 0
- residual: float32 [128, 64, 1024], P(('cycle', 'gx'), 'gy'), parts along dimension 0
There are 2 independent parts, one for each index of `cycle`. A program takes and returns all parts, laid end to end along the dimension named above; an argument that names none is the same for every part. Nothing has to cross between parts.
All inputs are finite; a program needn't handle non-finite values. No bound on the sum of `convection_flag` on one device may be relied on, other than what follows from the above.
Results may differ from a plain program's by a relative error of at most 0.00025.
Values sent between devices are 32-bit elements; how exact they have to be, the bound alone decides.
A program may use at most 64 MiB of HBM per device.

v0:
```python
import jax
import jax.numpy as jnp
from jax import lax
from jax.sharding import PartitionSpec as P

ITERS = 4


HCOOL = 1.5


def padded_2(cells, sides, width):
    for axis, dim in sides:
        count = lax.axis_size(axis)
        ends = count - 1
        head = lax.slice_in_dim(cells, 0, width, axis=dim)
        tail = lax.slice_in_dim(cells, cells.shape[dim] - width, cells.shape[dim], axis=dim)
        cells = jnp.concatenate(
            [
                lax.ppermute(tail, axis, [(i, (i + 1) % count) for i in range(ends)]),
                cells,
                lax.ppermute(head, axis, [((i + 1) % count, i) for i in range(ends)]),
            ],
            axis=dim,
        )
    return cells


def harmonic(near, far):
    return 2.0 * near * far / (near + far)


def substance_lookup(substance_label, table):
    result = jnp.zeros(substance_label.shape, jnp.float32)
    for index in range(table.shape[0]):
        result = result + jnp.where(substance_label == index, table[index], 0.0)
    return result


def beside_all(field):
    padded = padded_2(field, (("gx", 0), ("gy", 1)), 1)
    lower = padded[:-2, 1:-1]
    upper = padded[2:, 1:-1]
    left = padded[1:-1, :-2]
    right = padded[1:-1, 2:]
    deep = jnp.pad(field, ((0, 0), (0, 0), (1, 1)))
    return (lower, upper, left, right, deep[:, :, :-2], deep[:, :, 2:])


def operate(field, faces, diag):
    result = diag * field
    for face, near in zip(faces, beside_all(field)):
        result = result - face * near
    return result


def preconditioned_sum(residual_now, pre_now):
    return lax.psum(jnp.sum(residual_now * pre_now), ("gx", "gy"))


def per_device(
    stored_thermal_state,
    substance_label,
    convection_flag,
    adjoint_source,
    zero_kelvin_diffusivity,
    thermal_coefficient,
    thermal_storage_rate,
):
    voxel_diffusivity = substance_lookup(substance_label, zero_kelvin_diffusivity) * (
        1.0 + substance_lookup(substance_label, thermal_coefficient) * stored_thermal_state
    )
    base = substance_lookup(substance_label, thermal_storage_rate) + HCOOL * convection_flag.astype(
        jnp.float32
    )
    faces = tuple((harmonic(voxel_diffusivity, near) for near in beside_all(voxel_diffusivity)))
    diag = base
    for face in faces:
        diag = diag + face
    adjoint = jnp.zeros_like(adjoint_source)
    residual = adjoint_source
    pre = residual / diag
    direction = pre
    norm_now = preconditioned_sum(residual, pre)
    for step in range(ITERS):
        image = operate(direction, faces, diag)
        alpha = norm_now / lax.psum(jnp.sum(direction * image), ("gx", "gy"))
        adjoint = adjoint + alpha * direction
        residual = residual - alpha * image
        if step + 1 < ITERS:
            pre = residual / diag
            norm_next = preconditioned_sum(residual, pre)
            direction = pre + norm_next / norm_now * direction
            norm_now = norm_next
    return (adjoint, residual)


def solution(mesh):
    in_specs = (
        P(("cycle", "gx"), "gy", None),
        P("gx", "gy", None),
        P("gx", "gy", None),
        P(("cycle", "gx"), "gy", None),
        P(),
        P(),
        P(),
    )
    out_specs = (P(("cycle", "gx"), "gy", None), P(("cycle", "gx"), "gy", None))
    return jax.shard_map(
        per_device, mesh=mesh, in_specs=in_specs, out_specs=out_specs, check_vma=False
    )
```

profile of v0, /device:TPU:0, one launch (start us, length us, event | category | flops | bytes accessed | tf_op | source)
XLA Modules:
  0.0 357.6 jit_solution(1272856100731410888)
XLA Ops:
  3.9 13.5 %add_multiply_fusion = (f32[8,32,1024]{2,1,0:T(8,128)S(1)}, pred[8,32,1024]{2,1,0:T(8,128)(4,1)S(1)}, pred[8,32,1024]{2,1,0:T(8,128)(4,1)S(1)}, pred[8,32,1024]{...) fusion(f32[8,32,1024]{2,1,0:T(8,128)} %param.7, ...), kind=kLoop, calls=%fused_computation.125 | loop fusion | flops 10747904 | bytes 5242944 | tf_op jit(solution)/shard_map/mul | solution.py:70
  17.5 5.0 %collective-permute-start = (f32[1,32,1024]{2,1,0:T(8,128)S(1)}, f32[1,32,1024]{2,1,0:T(8,128)S(1)}, u32[]{:S(2)}, u32[]{:S(2)}) collective-permute-start(f32[1,32,1024]{2,1,0:T(8,128)S(1)} %get-tuple-element.53), channel_id=1, source_target_pairs={{0,2},{2,4},{4,6},{6,8},{8,10},{10,12},{12,14},{1,3},{3,5},{5,7},{... | collective-permute-start | bytes 393224 | tf_op jit(solution)/shard_map/ppermute | solution.py:20
  25.2 4.1 %collective-permute-done.1 = f32[1,32,1024]{2,1,0:T(8,128)S(1)} collective-permute-done((f32[1,32,1024]{2,1,0:T(8,128)S(1)}, f32[1,32,1024]{2,1,0:T(8,128)S(1)}, u32[]{:S(2)}, u32[]{:S(2)}) %collective-permute-start.1) | collective-permute-done | bytes 131104 | tf_op jit(solution)/shard_map/ppermute | solution.py:22
  33.8 7.9 %fusion.58 = (f32[8,32,1024]{2,1,0:T(8,128)S(1)}, f32[8,32,1024]{2,1,0:T(8,128)S(1)}, f32[8,32,1024]{2,1,0:T(8,128)S(1)}, f32[8,32,1024]{2,1,0:T(8,128)S(1)}) fusion(f32[8,32,1024]{2,1,0:T(8,128)S(1)} %copy-done.11, f32[8,32,1024]{2,1,0:T(8,128)S(1)} %get-tuple-element.26, f32[10,1,1024]{2,1,0:T(1,128)S(1)} %collective-permute-done.3, ...), kind=kLoop, calls=%fused_computation.149 | loop fusion | flops 13631488 | bytes 9781280 | tf_op jit(solution)/shard_map/div | solution.py:82
  41.8 4.3 %collective-permute-start.4 = (f32[1,32,1024]{2,1,0:T(8,128)S(1)}, f32[1,32,1024]{2,1,0:T(8,128)S(1)}, u32[]{:S(2)}, u32[]{:S(2)}) collective-permute-start(f32[1,32,1024]{2,1,0:T(8,128)S(1)} %get-tuple-element.51), channel_id=1, source_target_pairs={{0,2},{2,4},{4,6},{6,8},{8,10},{10,12},{12,14},{1,3},{3,5},{5,7},{... | collective-permute-start | bytes 393224 | tf_op jit(solution)/shard_map/ppermute | solution.py:20
  49.2 4.1 %collective-permute-done.5 = f32[1,32,1024]{2,1,0:T(8,128)S(1)} collective-permute-done((f32[1,32,1024]{2,1,0:T(8,128)S(1)}, f32[1,32,1024]{2,1,0:T(8,128)S(1)}, u32[]{:S(2)}, u32[]{:S(2)}) %collective-permute-start.5) | collective-permute-done | bytes 131104 | tf_op jit(solution)/shard_map/ppermute | solution.py:22
  57.8 3.9 %multiply_reduce_fusion.6 = (f32[]{:T(128)}, f32[]{:T(128)}, f32[8,32,1024]{2,1,0:T(8,128)}) fusion(f32[8,32,1024]{2,1,0:T(8,128)S(1)} %get-tuple-element.22, f32[8,32,1024]{2,1,0:T(8,128)S(1)} %copy-done.11, f32[8,32,1024]{2,1,0:T(8,128)S(1)} %get-tuple-element.24, f32[8,32,1024]{2,1,0:T(8,128)S(1)} %get-tuple-element.25, ...), kind=kLoop, calls=%fused_computation.118 | loop fusion | flops 12058622 | bytes 8028168 | tf_op jit(solution)/shard_map/reduce_sum | solution.py:87
  61.7 33.3 %all-reduce.5 = (f32[]{:T(128)}, f32[]{:T(128)}) all-reduce(f32[]{:T(128)} %get-tuple-element.3, f32[]{:T(128)} %get-tuple-element.2), channel_id=1, replica_groups=mesh['cycle'=2,'gx'=8,'gy'=2] {'gx','gy'}, use_global_device_ids=true, to_apply=%region_1.2 | all-reduce | flops 2 | bytes 16 | tf_op jit(solution)/shard_map/psum | solution.py:58
  96.3 3.9 %multiply_reduce_fusion.5 = (f32[]{:T(128)}, f32[8,32,1024]{2,1,0:T(8,128)}, f32[8,32,1024]{2,1,0:T(8,128)}) fusion(f32[8,32,1024]{2,1,0:T(8,128)S(1)} %get-tuple-element.23, f32[8,32,1024]{2,1,0:T(8,128)} %param.10, f32[8,32,1024]{2,1,0:T(8,128)} %get-tuple-element.21, f32[]{:T(128)S(6)} %div.58), kind=kLoop, calls=%fused_computation.116 | loop fusion | flops 1310719 | bytes 5242888 | tf_op jit(solution)/shard_map/reduce_sum | solution.py:58
  100.3 30.1 %psum.58 = f32[]{:T(128)} all-reduce(f32[]{:T(128)} %get-tuple-element.18), channel_id=1, replica_groups=mesh['cycle'=2,'gx'=8,'gy'=2] {'gx','gy'}, use_global_device_ids=true, to_apply=%region_5.6 | all-reduce | flops 1 | bytes 8 | tf_op jit(solution)/shard_map/psum | solution.py:58
  135.9 4.5 %collective-permute-done.8 = f32[1,32,1024]{2,1,0:T(8,128)S(1)} collective-permute-done((f32[1,32,1024]{2,1,0:T(8,128)S(1)}, f32[1,32,1024]{2,1,0:T(8,128)S(1)}, u32[]{:S(2)}, u32[]{:S(2)}) %collective-permute-start.8) | collective-permute-done | bytes 131104 | tf_op jit(solution)/shard_map/ppermute | solution.py:20
  146.3 3.8 %multiply_reduce_fusion.4 = (f32[]{:T(128)}, f32[8,32,1024]{2,1,0:T(8,128)}) fusion(f32[8,32,1024]{2,1,0:T(8,128)S(1)} %multiply_add_fusion.3, f32[8,32,1024]{2,1,0:T(8,128)S(1)} %copy-done.3, f32[8,32,1024]{2,1,0:T(8,128)S(1)} %copy-done.7, f32[10,1,1024]{2,1,0:T(1,128)S(1)} %collective-permute-done.11, f32[1,32,1024]{2,1,0:T(8,128)S(1)} %collective-permute-done.9, ...), kind=kLoop, calls=%fused_computation.114 | loop fusion | flops 11534335 | bytes 6979588 | tf_op jit(solution)/shard_map/reduce_sum | solution.py:87
  150.1 30.2 %psum.59 = f32[]{:T(128)} all-reduce(f32[]{:T(128)} %get-tuple-element.16), channel_id=1, replica_groups=mesh['cycle'=2,'gx'=8,'gy'=2] {'gx','gy'}, use_global_device_ids=true, to_apply=%region_7.8 | all-reduce | flops 1 | bytes 8 | tf_op jit(solution)/shard_map/psum | solution.py:87
  181.6 4.0 %multiply_reduce_fusion.3 = (f32[]{:T(128)}, f32[8,32,1024]{2,1,0:T(8,128)}, f32[8,32,1024]{2,1,0:T(8,128)}) fusion(f32[8,32,1024]{2,1,0:T(8,128)S(1)} %get-tuple-element.23, f32[8,32,1024]{2,1,0:T(8,128)} %get-tuple-element.20, f32[8,32,1024]{2,1,0:T(8,128)} %get-tuple-element.17, f32[]{:T(128)S(6)} %div.61), kind=kLoop, calls=%fused_computation.112 | loop fusion | flops 1310719 | bytes 5242888 | tf_op jit(solution)/shard_map/reduce_sum | solution.py:58
  185.5 30.2 %psum.60 = f32[]{:T(128)} all-reduce(f32[]{:T(128)} %get-tuple-element.13), channel_id=1, replica_groups=mesh['cycle'=2,'gx'=8,'gy'=2] {'gx','gy'}, use_global_device_ids=true, to_apply=%region_9.10 | all-reduce | flops 1 | bytes 8 | tf_op jit(solution)/shard_map/psum | solution.py:58
  221.6 4.5 %collective-permute-done.12 = f32[1,32,1024]{2,1,0:T(8,128)S(1)} collective-permute-done((f32[1,32,1024]{2,1,0:T(8,128)S(1)}, f32[1,32,1024]{2,1,0:T(8,128)S(1)}, u32[]{:S(2)}, u32[]{:S(2)}) %collective-permute-start.12) | collective-permute-done | bytes 131104 | tf_op jit(solution)/shard_map/ppermute | solution.py:20
  232.0 3.7 %multiply_reduce_fusion.2 = (f32[]{:T(128)}, f32[8,32,1024]{2,1,0:T(8,128)}) fusion(f32[8,32,1024]{2,1,0:T(8,128)S(1)} %multiply_add_fusion.2, f32[8,32,1024]{2,1,0:T(8,128)S(1)} %copy-done.4, f32[8,32,1024]{2,1,0:T(8,128)S(1)} %copy-done.8, f32[10,1,1024]{2,1,0:T(1,128)S(1)} %collective-permute-done.15, f32[1,32,1024]{2,1,0:T(8,128)S(1)} %collective-permute-done.13, ...), kind=kLoop, calls=%fused_computation.110 | loop fusion | flops 11534335 | bytes 6979588 | tf_op jit(solution)/shard_map/reduce_sum | solution.py:87
  235.7 30.2 %psum.61 = f32[]{:T(128)} all-reduce(f32[]{:T(128)} %get-tuple-element.11), channel_id=1, replica_groups=mesh['cycle'=2,'gx'=8,'gy'=2] {'gx','gy'}, use_global_device_ids=true, to_apply=%region_11.12 | all-reduce | flops 1 | bytes 8 | tf_op jit(solution)/shard_map/psum | solution.py:87
  267.3 3.9 %multiply_reduce_fusion.1 = (f32[]{:T(128)}, f32[8,32,1024]{2,1,0:T(8,128)}, f32[8,32,1024]{2,1,0:T(8,128)}) fusion(f32[8,32,1024]{2,1,0:T(8,128)S(1)} %get-tuple-element.23, f32[8,32,1024]{2,1,0:T(8,128)} %get-tuple-element.15, f32[8,32,1024]{2,1,0:T(8,128)} %get-tuple-element.12, f32[]{:T(128)S(6)} %div.64), kind=kLoop, calls=%fused_computation.108 | loop fusion | flops 1310719 | bytes 5242888 | tf_op jit(solution)/shard_map/reduce_sum | solution.py:58
  271.2 30.1 %psum.62 = f32[]{:T(128)} all-reduce(f32[]{:T(128)} %get-tuple-element.8), channel_id=1, replica_groups=mesh['cycle'=2,'gx'=8,'gy'=2] {'gx','gy'}, use_global_device_ids=true, to_apply=%region_13.14 | all-reduce | flops 1 | bytes 8 | tf_op jit(solution)/shard_map/psum | solution.py:58
  307.2 4.5 %collective-permute-done.16 = f32[1,32,1024]{2,1,0:T(8,128)S(1)} collective-permute-done((f32[1,32,1024]{2,1,0:T(8,128)S(1)}, f32[1,32,1024]{2,1,0:T(8,128)S(1)}, u32[]{:S(2)}, u32[]{:S(2)}) %collective-permute-start.16) | collective-permute-done | bytes 131104 | tf_op jit(solution)/shard_map/ppermute | solution.py:20
  317.6 3.8 %multiply_reduce_fusion = (f32[]{:T(128)}, f32[8,32,1024]{2,1,0:T(8,128)}) fusion(f32[8,32,1024]{2,1,0:T(8,128)S(1)} %multiply_add_fusion.1, f32[8,32,1024]{2,1,0:T(8,128)S(1)} %copy-done.5, f32[8,32,1024]{2,1,0:T(8,128)S(1)} %copy-done.9, f32[10,1,1024]{2,1,0:T(1,128)S(1)} %collective-permute-done.19, f32[1,32,1024]{2,1,0:T(8,128)S(1)} %collective-permute-done.17, ...), kind=kLoop, calls=%fused_computation.106 | loop fusion | flops 11534335 | bytes 6979588 | tf_op jit(solution)/shard_map/reduce_sum | solution.py:87
  321.4 30.2 %psum.63 = f32[]{:T(128)} all-reduce(f32[]{:T(128)} %get-tuple-element.6), channel_id=1, replica_groups=mesh['cycle'=2,'gx'=8,'gy'=2] {'gx','gy'}, use_global_device_ids=true, to_apply=%region_15.16 | all-reduce | flops 1 | bytes 8 | tf_op jit(solution)/shard_map/psum | solution.py:87
  352.8 4.8 %multiply_subtract_fusion = (f32[8,32,1024]{2,1,0:T(8,128)}, f32[8,32,1024]{2,1,0:T(8,128)}) fusion(f32[8,32,1024]{2,1,0:T(8,128)} %get-tuple-element.10, f32[8,32,1024]{2,1,0:T(8,128)} %get-tuple-element.7, f32[]{:T(128)S(6)} %div.67, f32[8,32,1024]{2,1,0:T(8,128)} %copy-done.10, f32[8,32,1024]{2,1,0:T(8,128)} %copy-done.1, f32[]{:T(128)S(6)} %div.64, ...), kind=kLoop, calls=%fused_computation.104 | loop fusion | flops 2359296 | bytes 8388624 | tf_op jit(solution)/shard_map/sub | solution.py:89
  (77 shorter events, 48.6 us)
Async XLA Ops:
  3.9 29.9 %copy-start.12 = (s32[8,32,1024]{2,1,0:T(8,128)S(1)}, s32[8,32,1024]{2,1,0:T(8,128)}, u32[]{:S(2)}) copy-start(s32[8,32,1024]{2,1,0:T(8,128)} %param.9) | copy-start | bytes 3145732
  17.5 7.7 %collective-permute-start = (f32[1,32,1024]{2,1,0:T(8,128)S(1)}, f32[1,32,1024]{2,1,0:T(8,128)S(1)}, u32[]{:S(2)}, u32[]{:S(2)}) collective-permute-start(f32[1,32,1024]{2,1,0:T(8,128)S(1)} %get-tuple-element.53), channel_id=1, source_target_pairs={{0,2},{2,4},{4,6},{6,8},{8,10},{10,12},{12,14},{1,3},{3,5},{5,7},{... | collective-permute-start | bytes 393224 | tf_op jit(solution)/shard_map/ppermute | solution.py:20
  22.5 6.9 %collective-permute-start.1 = (f32[1,32,1024]{2,1,0:T(8,128)S(1)}, f32[1,32,1024]{2,1,0:T(8,128)S(1)}, u32[]{:S(2)}, u32[]{:S(2)}) collective-permute-start(f32[1,32,1024]{2,1,0:T(8,128)S(1)} %get-tuple-element.54), channel_id=1, source_target_pairs={{2,0},{4,2},{6,4},{8,6},{10,8},{12,10},{14,12},{3,1},{5,3},{7,5},{... | collective-permute-start | bytes 393224 | tf_op jit(solution)/shard_map/ppermute | solution.py:22
  29.4 3.3 collective-permute-start.2
  30.7 3.1 collective-permute-start.3
  41.7 19.9 %copy-start.2 = (f32[8,32,1024]{2,1,0:T(8,128)}, f32[8,32,1024]{2,1,0:T(8,128)S(1)}, u32[]{:S(2)}) copy-start(f32[8,32,1024]{2,1,0:T(8,128)S(1)} %get-tuple-element.24) | copy-start | bytes 3145732
  41.8 19.9 %copy-start.6 = (f32[8,32,1024]{2,1,0:T(8,128)}, f32[8,32,1024]{2,1,0:T(8,128)S(1)}, u32[]{:S(2)}) copy-start(f32[8,32,1024]{2,1,0:T(8,128)S(1)} %get-tuple-element.25) | copy-start | bytes 3145732
  41.8 7.4 %collective-permute-start.4 = (f32[1,32,1024]{2,1,0:T(8,128)S(1)}, f32[1,32,1024]{2,1,0:T(8,128)S(1)}, u32[]{:S(2)}, u32[]{:S(2)}) collective-permute-start(f32[1,32,1024]{2,1,0:T(8,128)S(1)} %get-tuple-element.51), channel_id=1, source_target_pairs={{0,2},{2,4},{4,6},{6,8},{8,10},{10,12},{12,14},{1,3},{3,5},{5,7},{... | collective-permute-start | bytes 393224 | tf_op jit(solution)/shard_map/ppermute | solution.py:20
  46.1 7.2 %collective-permute-start.5 = (f32[1,32,1024]{2,1,0:T(8,128)S(1)}, f32[1,32,1024]{2,1,0:T(8,128)S(1)}, u32[]{:S(2)}, u32[]{:S(2)}) collective-permute-start(f32[1,32,1024]{2,1,0:T(8,128)S(1)} %get-tuple-element.52), channel_id=1, source_target_pairs={{2,0},{4,2},{6,4},{8,6},{10,8},{12,10},{14,12},{3,1},{5,3},{7,5},{... | collective-permute-start | bytes 393224 | tf_op jit(solution)/shard_map/ppermute | solution.py:22
  53.4 2.6 collective-permute-start.6
  54.7 3.1 collective-permute-start.7
  133.2 17.0 %copy-start = (f32[8,32,1024]{2,1,0:T(8,128)}, f32[8,32,1024]{2,1,0:T(8,128)S(1)}, u32[]{:S(2)}) copy-start(f32[8,32,1024]{2,1,0:T(8,128)S(1)} %multiply_add_fusion.3) | copy-start | bytes 3145732
  133.2 7.3 %collective-permute-start.8 = (f32[1,32,1024]{2,1,0:T(8,128)S(1)}, f32[1,32,1024]{2,1,0:T(8,128)S(1)}, u32[]{:S(2)}, u32[]{:S(2)}) collective-permute-start(f32[1,32,1024]{2,1,0:T(8,128)S(1)} %get-tuple-element.49), channel_id=1, source_target_pairs={{0,2},{2,4},{4,6},{6,8},{8,10},{10,12},{12,14},{1,3},{3,5},{5,7},{... | collective-permute-start | bytes 393224 | tf_op jit(solution)/shard_map/ppermute | solution.py:20
  134.6 7.2 %collective-permute-start.9 = (f32[1,32,1024]{2,1,0:T(8,128)S(1)}, f32[1,32,1024]{2,1,0:T(8,128)S(1)}, u32[]{:S(2)}, u32[]{:S(2)}) collective-permute-start(f32[1,32,1024]{2,1,0:T(8,128)S(1)} %get-tuple-element.50), channel_id=1, source_target_pairs={{2,0},{4,2},{6,4},{8,6},{10,8},{12,10},{14,12},{3,1},{5,3},{7,5},{... | collective-permute-start | bytes 393224 | tf_op jit(solution)/shard_map/ppermute | solution.py:22
  141.9 2.6 collective-permute-start.10
  143.2 3.1 collective-permute-start.11
  218.9 7.3 %collective-permute-start.12 = (f32[1,32,1024]{2,1,0:T(8,128)S(1)}, f32[1,32,1024]{2,1,0:T(8,128)S(1)}, u32[]{:S(2)}, u32[]{:S(2)}) collective-permute-start(f32[1,32,1024]{2,1,0:T(8,128)S(1)} %get-tuple-element.47), channel_id=1, source_target_pairs={{0,2},{2,4},{4,6},{6,8},{8,10},{10,12},{12,14},{1,3},{3,5},{5,7},{... | collective-permute-start | bytes 393224 | tf_op jit(solution)/shard_map/ppermute | solution.py:20
  220.3 7.2 %collective-permute-start.13 = (f32[1,32,1024]{2,1,0:T(8,128)S(1)}, f32[1,32,1024]{2,1,0:T(8,128)S(1)}, u32[]{:S(2)}, u32[]{:S(2)}) collective-permute-start(f32[1,32,1024]{2,1,0:T(8,128)S(1)} %get-tuple-element.48), channel_id=1, source_target_pairs={{2,0},{4,2},{6,4},{8,6},{10,8},{12,10},{14,12},{3,1},{5,3},{7,5},{... | collective-permute-start | bytes 393224 | tf_op jit(solution)/shard_map/ppermute | solution.py:22
  227.6 2.6 collective-permute-start.14
  228.9 3.1 collective-permute-start.15
  304.5 7.3 %collective-permute-start.16 = (f32[1,32,1024]{2,1,0:T(8,128)S(1)}, f32[1,32,1024]{2,1,0:T(8,128)S(1)}, u32[]{:S(2)}, u32[]{:S(2)}) collective-permute-start(f32[1,32,1024]{2,1,0:T(8,128)S(1)} %get-tuple-element.45), channel_id=1, source_target_pairs={{0,2},{2,4},{4,6},{6,8},{8,10},{10,12},{12,14},{1,3},{3,5},{5,7},{... | collective-permute-start | bytes 393224 | tf_op jit(solution)/shard_map/ppermute | solution.py:20
  305.9 7.2 %collective-permute-start.17 = (f32[1,32,1024]{2,1,0:T(8,128)S(1)}, f32[1,32,1024]{2,1,0:T(8,128)S(1)}, u32[]{:S(2)}, u32[]{:S(2)}) collective-permute-start(f32[1,32,1024]{2,1,0:T(8,128)S(1)} %get-tuple-element.46), channel_id=1, source_target_pairs={{2,0},{4,2},{6,4},{8,6},{10,8},{12,10},{14,12},{3,1},{5,3},{7,5},{... | collective-permute-start | bytes 393224 | tf_op jit(solution)/shard_map/ppermute | solution.py:22
  313.1 2.6 collective-permute-start.18
  314.4 3.1 collective-permute-start.19
  (10 other events, 148.6 us)
where the time goes:
time: 359 us; the launch traced here: 358 us
  blocking collectives  214 us (60%)
  other arithmetic  58.6 us (16%)
  waiting for transfers between devices  37.3 us (10%)
  starting transfers between devices  33 us (9%)
  between operations  10.1 us (3%)
  local copies, waits for them, and re-layouts  4.11 us (1%)
    psum x4, blocking collectives, preconditioned_sum(): return lax.psum(jnp.sum(residual_now * pre_now), ('gx', 'gy'))  124 us
    psum x3, blocking collectives, per_device(): alpha = norm_now / lax.psum(jnp.sum(direction * image), ('gx', 'gy'))  90.7 us
    ppermute x10, waiting for transfers between devices, padded_2(): lax.ppermute(head, axis, [((i + 1) % count, i) for i in range(ends)])  20.5 us
    ppermute x10, starting transfers between devices, padded_2(): lax.ppermute(tail, axis, [(i, (i + 1) % count) for i in range(ends)])  20.1 us
    ppermute x10, waiting for transfers between devices, padded_2(): lax.ppermute(tail, axis, [(i, (i + 1) % count) for i in range(ends)])  16.8 us
    reduce_sum x4, other arithmetic, per_device(): alpha = norm_now / lax.psum(jnp.sum(direction * image), ('gx', 'gy'))  15.2 us
    mul x1, other arithmetic, per_device(): substance_lookup(substance_label, zero_kelvin_diffusivity)  13.5 us
    ppermute x10, starting transfers between devices, padded_2(): lax.ppermute(head, axis, [((i + 1) % count, i) for i in range(ends)])  12.9 us
  transfers between devices with their start and end apart: 20, of which 15 were waited for; matrix products, arithmetic and copies ran while one was open for 0% of the time, Pallas kernels for 0%

commit v1 on v0

v1 whole, which is shorter than its diff:
```python
import functools

import jax
import jax.numpy as jnp
from jax import lax
from jax.experimental import pallas as pl
from jax.experimental.pallas import tpu as pltpu
from jax.sharding import PartitionSpec as P

HCOOL = 1.5
STEPS = 4
PAD = 8
MESH = pl.DeviceIdType.MESH


def fold(x):
    total = x[:, :128]
    for lane in range(128, x.shape[1], 128):
        total = total + x[:, lane : lane + 128]
    return total


def harmonic(a, b):
    return 2.0 * a * b / (a + b)


def spread(x):
    return jnp.broadcast_to(jnp.sum(x, axis=(0, 1), keepdims=True), (8, 128))


def kernel(
    ngx, ngy, cuts,
    temp_hbm, label_hbm, flag_hbm, source_hbm, k0_ref, tc_ref, ts_ref,
    adjoint_ref, residual_ref,
    temp, label, flag, source, cond, v0, v1, v2, v3, v4,
    face_row, face_left, face_right, face_down, face_up, inv, diag,
    edge_out, edge_in, part_out, part_in,
    load_sem, row_send, row_recv, edge_send, edge_recv, part_send, part_recv,
):
    rows, cols, depth = temp.shape
    tiles = cols // 8
    gx, gy = lax.axis_index("gx"), lax.axis_index("gy")
    n = ngx * ngy
    me = gx * ngy + gy
    fields = (cond, v0, v1, v2, v3, v4)
    v = fields[1:]
    has_lower, has_upper = gx > 0, gx < ngx - 1

    def peer(offset):
        p = lax.rem(me + offset, n)
        return {"gx": p // ngy, "gy": lax.rem(p, ngy)}

    def load(a, group):
        src, dst = ((temp_hbm, temp), (label_hbm, label), (source_hbm, source), (flag_hbm, flag))[a]
        first, size = ((0, 1), (rows - 1, 1), (1, rows - 2))[group]
        return pltpu.make_async_copy(
            src.at[pl.ds(first, size)], dst.at[pl.ds(first, size)], load_sem.at[a, group]
        )

    order = [(a, g) for a in (0, 1) for g in (0, 1)] + [(a, g) for a in (2, 3) for g in (0, 1)]
    order += [(a, 2) for a in range(4)]
    for a, g in order:
        load(a, g).start()

    barrier = pltpu.get_barrier_semaphore()

    def greet(offset, carry):
        pl.semaphore_signal(barrier, inc=1, device_id=peer(offset), device_id_type=MESH)
        return carry

    lax.fori_loop(1, n, greet, 0)

    zero_row = jnp.zeros((cols, depth), jnp.float32)
    zero_edge = jnp.zeros((8, depth), jnp.float32)

    @pl.when(jnp.logical_not(has_lower))
    def _():
        for field in fields[:-1]:
            field[0, PAD : PAD + cols, :] = zero_row

    @pl.when(jnp.logical_not(has_upper))
    def _():
        for field in fields[:-1]:
            field[rows + 1, PAD : PAD + cols, :] = zero_row

    for field in fields[:-1]:
        for i in range(1, rows + 1):
            field[i, 0:PAD, :] = zero_edge
            field[i, PAD + cols : PAD + cols + 8, :] = zero_edge
    for k in range(STEPS + 1):
        edge_out[k, 0:8, :] = zero_edge
        edge_out[k, 8:16, :] = zero_edge

    width = cols // cuts
    own_edge = jnp.where(gy == 0, PAD + cols - 1, PAD)
    halo_edge = jnp.where(gy == 0, PAD + cols, PAD - 1)

    def row_copy(k, side, c):
        src, dst = ((1, rows + 1), (rows, 0))[side]
        part = pl.ds(PAD + c * width, width)
        return pltpu.make_async_remote_copy(
            src_ref=fields[k].at[src, part, :],
            dst_ref=fields[k].at[dst, part, :],
            send_sem=row_send.at[k, side, c],
            recv_sem=row_recv.at[k, side, c],
            device_id={"gx": gx - 1 if side == 0 else gx + 1},
            device_id_type=MESH,
        )

    def has(side):
        return has_lower if side == 0 else has_upper

    def send_row(k, side, c):
        @pl.when(has(side))
        def _():
            row_copy(k, side, c).start()

    def wait_row(k, end, c):
        @pl.when(has(end))
        def _():
            row_copy(k, 1 - end, c).wait_recv()

    def edge_copy(k, group):
        part = pl.ds(8 * group, 8)
        return pltpu.make_async_remote_copy(
            src_ref=edge_out.at[k, part, :],
            dst_ref=edge_in.at[k, part, :],
            send_sem=edge_send.at[k, group],
            recv_sem=edge_recv.at[k, group],
            device_id={"gy": 1 - gy},
            device_id_type=MESH,
        )

    spots = ([(1, 0), (rows, 1)], [(i, 8 + i - 2) for i in range(2, rows)])

    def send_edge(k, group):
        for i, spot in spots[group]:
            edge_out[k, spot : spot + 1, :] = fields[k][i, pl.ds(own_edge, 1), :]
        edge_copy(k, group).start()

    def wait_edge(k, group):
        edge_copy(k, group).wait_recv()
        for i, spot in spots[group]:
            fields[k][i, pl.ds(halo_edge, 1), :] = edge_in[k, spot : spot + 1, :]

    def table(ref, marks):
        out = jnp.zeros(marks[0].shape, jnp.float32)
        for m, mark in enumerate(marks):
            out = jnp.where(mark, ref[m], out)
        return out

    def conduct(i, t):
        part = pl.ds(8 * t, 8)
        kind = label[i - 1, part, :]
        marks = [kind == m for m in range(k0_ref.shape[0])]
        cond[i, pl.ds(PAD + 8 * t, 8), :] = table(k0_ref, marks) * (
            1.0 + table(tc_ref, marks) * temp[i - 1, part, :]
        )

    def start_row(i, t, end):
        at = PAD + 8 * t
        part = pl.ds(8 * t, 8)
        c = cond[i, pl.ds(at, 8), :]
        lower = harmonic(c, cond[i - 1, pl.ds(at, 8), :])
        upper = harmonic(c, cond[i + 1, pl.ds(at, 8), :])
        left = harmonic(c, cond[i, pl.ds(at - 1, 8), :])
        right = harmonic(c, cond[i, pl.ds(at + 1, 8), :])
        lane = lax.broadcasted_iota(jnp.int32, c.shape, 1)
        down = harmonic(c, jnp.where(lane == 0, 0.0, pltpu.roll(c, 1, 1)))
        up = pltpu.roll(down, depth - 1, 1)
        face_row[i - 1, part, :] = lower
        face_row[i, part, :] = upper
        face_left[i - 1, part, :] = left
        face_right[i - 1, part, :] = right
        face_down[i - 1, part, :] = down
        face_up[i - 1, part, :] = up
        kind = label[i - 1, part, :]
        marks = [kind == m for m in range(k0_ref.shape[0])]
        base = table(ts_ref, marks) + HCOOL * flag[i - 1, part, :].astype(jnp.float32)
        d = base + lower + upper + left + right + down + up
        s = source[i - 1, part, :]
        over = 1.0 / d
        diag[i - 1, part, :] = d
        inv[i - 1, part, :] = over
        z = s * over
        v0[i, pl.ds(at, 8), :] = z
        return fold(z * s)

    def apply(k, i, t):
        at = PAD + 8 * t
        part = pl.ds(8 * t, 8)
        field = v[k]
        x = field[i, pl.ds(at, 8), :]
        w = face_row[i - 1, part, :] * field[i - 1, pl.ds(at, 8), :]
        w += face_row[i, part, :] * field[i + 1, pl.ds(at, 8), :]
        w += face_left[i - 1, part, :] * field[i, pl.ds(at - 1, 8), :]
        w += face_right[i - 1, part, :] * field[i, pl.ds(at + 1, 8), :]
        w += face_down[i - 1, part, :] * pltpu.roll(x, 1, 1)
        w += face_up[i - 1, part, :] * pltpu.roll(x, depth - 1, 1)
        y = w * inv[i - 1, part, :]
        v[k + 1][i, pl.ds(at, 8), :] = y
        return w, x, y

    zero = jnp.zeros((8, 128), jnp.float32)
    lane128 = lax.broadcasted_iota(jnp.int32, (8, 128), 1)

    def part_copy(which, offset):
        return pltpu.make_async_remote_copy(
            src_ref=part_out.at[which],
            dst_ref=part_in.at[which, offset],
            send_sem=part_send.at[which, offset],
            recv_sem=part_recv.at[which, offset],
            device_id=peer(offset),
            device_id_type=MESH,
        )

    def send_parts(which, sums):
        tile = zero
        for d, s in enumerate(sums):
            tile = jnp.where(lane128 == d, jnp.sum(s, axis=(0, 1), keepdims=True), tile)
        part_out[which] = tile

        def one(offset, carry):
            part_copy(which, offset).start()
            return carry

        lax.fori_loop(1, n, one, 0)

    def take_parts(which, count):
        part_in[which, 0] = part_out[which]

        def wait(offset, carry):
            part_copy(which, offset).wait_recv()
            return carry

        lax.fori_loop(1, n, wait, 0)

        def add(p, tile):
            return tile + part_in[which, lax.rem(me - p + n, n)]

        tile = lax.fori_loop(0, n, add, zero)
        return [
            jnp.broadcast_to(
                jnp.sum(jnp.where(lane128 == d, tile, 0.0), axis=1, keepdims=True), (8, 128)
            )
            for d in range(count)
        ]

    def tiles_of(c):
        return range(c * width // 8, (c + 1) * width // 8)

    ends = ((0, 1), (1, rows))

    for a in (0, 1):
        for g in (0, 1):
            load(a, g).wait()
    for end, i in ends:
        for t in range(tiles):
            conduct(i, t)
    pl.semaphore_wait(barrier, n - 1)
    for c in range(cuts):
        for end, i in ends:
            send_row(0, end, c)
    send_edge(0, 0)
    load(0, 2).wait()
    load(1, 2).wait()

    def conduct_row(i, carry):
        for t in range(tiles):
            conduct(i, t)
        return carry

    lax.fori_loop(2, rows, conduct_row, 0)
    send_edge(0, 1)

    for a in (2, 3):
        for g in (0, 1):
            load(a, g).wait()
    wait_edge(0, 0)
    sums = [zero]
    for c in range(cuts):
        for end, i in ends:
            wait_row(0, end, c)
            for t in tiles_of(c):
                sums[0] = sums[0] + start_row(i, t, end)
            send_row(1, end, c)
    send_edge(1, 0)
    load(2, 2).wait()
    load(3, 2).wait()
    wait_edge(0, 1)

    def start_rows(i, acc):
        for t in range(tiles):
            acc = acc + start_row(i, t, None)
        return acc

    sums[0] = lax.fori_loop(2, rows, start_rows, sums[0])
    send_edge(1, 1)

    theta = bend = shift = gain = None
    for k in range(STEPS):
        last = k == STEPS - 1

        def visit(i, t, acc, k=k):
            w, x, y = apply(k, i, t)
            if k < 2:
                return (acc[0] + fold(w * x), acc[1] + fold(w * y))
            return acc

        acc = (zero, zero)
        wait_edge(k + 1, 0)
        for c in range(cuts):
            for end, i in ends:
                wait_row(k + 1, end, c)
                for t in tiles_of(c):
                    acc = visit(i, t, acc)
                if not last:
                    send_row(k + 2, end, c)
        if not last:
            send_edge(k + 2, 0)
        wait_edge(k + 1, 1)

        def visit_row(i, acc, visit=visit):
            for t in range(tiles):
                acc = visit(i, t, acc)
            return acc

        acc = lax.fori_loop(2, rows, visit_row, acc)
        if not last:
            send_edge(k + 2, 1)
        if k < 2:
            sums += list(acc)
        if k == 1:
            send_parts(0, sums)
        if k == 2:
            m = take_parts(0, 5)
            theta = m[1] / m[0]
            size = m[2] - theta * m[1]
            gain = jnp.maximum(size / m[0], 0.0)
            turn = m[3] - 2.0 * theta * m[2] + theta * theta * m[1]
            shift = jnp.where(size > 0.0, turn / jnp.where(size > 0.0, size, 1.0), 0.0)
            shift = jnp.minimum(jnp.maximum(shift, -1.0), 1.0)
            bend = shift * theta - gain
            slope = -(shift + theta)

    wide = lambda x: x[:, 0:1] * jnp.ones((1, depth), jnp.float32)
    theta_w, slope_w, bend_w = wide(theta), wide(slope), wide(bend)
    pairs = [(a, b) for a in range(4) for b in range(a, 5)]

    def gram_row(i, acc):
        acc = list(acc)
        for t in range(tiles):
            at = pl.ds(PAD + 8 * t, 8)
            f = [u[i, at, :] for u in v]
            d = diag[i - 1, pl.ds(8 * t, 8), :]
            q = [
                f[0],
                f[1] - theta_w * f[0],
                f[2] + slope_w * f[1] + bend_w * f[0],
                f[3] + slope_w * f[2] + bend_w * f[1],
                f[4] + slope_w * f[3] + bend_w * f[2],
            ]
            for a in range(4):
                dq = d * q[a]
                for b in range(a, 5):
                    spot = pairs.index((a, b))
                    acc[spot] = acc[spot] + fold(dq * q[b])
        return tuple(acc)

    grams = lax.fori_loop(1, rows + 1, gram_row, (zero,) * len(pairs))
    send_parts(1, grams)
    m = take_parts(1, len(pairs))
    gram = {}
    for (a, b), value in zip(pairs, m):
        gram[a, b] = gram[b, a] = value

    def times(p):
        out = [None] * 5
        def put(j, x):
            out[j] = x if out[j] is None else out[j] + x
        if p[0] is not None:
            put(0, theta * p[0])
            put(1, p[0])
        if p[1] is not None:
            put(0, gain * p[1])
            put(1, shift * p[1])
            put(2, p[1])
        if p[2] is not None:
            put(3, p[2])
        if p[3] is not None:
            put(4, p[3])
        return out

    def add(a, b, scale):
        out = []
        for x, y in zip(a, b):
            if y is None:
                out.append(x)
            elif x is None:
                out.append(scale * y)
            else:
                out.append(x + scale * y)
        return out

    def inner(a, b):
        total = None
        for i, x in enumerate(a):
            if x is None:
                continue
            line = None
            for j, y in enumerate(b):
                if y is not None:
                    term = gram[i, j] * y
                    line = term if line is None else line + term
            total = x * line if total is None else total + x * line
        return total

    one = jnp.ones((8, 128), jnp.float32)
    adj, res, way = [None] * 5, [one] + [None] * 4, [one] + [None] * 4
    norm = gram[0, 0]
    for step in range(STEPS):
        image = add(way, times(way), -one)
        alpha = norm / inner(way, image)
        adj = add(adj, way, alpha)
        res = add(res, image, -alpha)
        if step + 1 < STEPS:
            after = inner(res, res)
            way = add(res, way, after / norm)
            norm = after

    def back(q):
        q = [zero if x is None else x for x in q]
        return [
            q[0] - theta * q[1] + bend * q[2],
            q[1] + slope * q[2] + bend * q[3],
            q[2] + slope * q[3] + bend * q[4],
            q[3] + slope * q[4],
            q[4],
        ]

    adj_w = [wide(x) for x in back(adj)[:4]]
    res_w = [wide(x) for x in back(res)]

    def finish_row(i, carry):
        for t in range(tiles):
            at = pl.ds(PAD + 8 * t, 8)
            part = pl.ds(8 * t, 8)
            f = [u[i, at, :] for u in v]
            x = adj_w[0] * f[0]
            for j in range(1, 4):
                x += adj_w[j] * f[j]
            r = res_w[0] * f[0]
            for j in range(1, 5):
                r += res_w[j] * f[j]
            adjoint_ref[i - 1, part, :] = x
            residual_ref[i - 1, part, :] = r * diag[i - 1, part, :]
        return carry

    lax.fori_loop(1, rows + 1, finish_row, 0)

    for k in range(STEPS + 1):
        for group in (0, 1):
            edge_copy(k, group).wait_send()
        for side in (0, 1):
            @pl.when(has(side))
            def _(k=k, side=side):
                for c in range(cuts):
                    row_copy(k, side, c).wait_send()

    def sent(offset, carry):
        for which in (0, 1):
            part_copy(which, offset).wait_send()
        return carry

    lax.fori_loop(1, n, sent, 0)


def per_device(ngx, ngy, cuts, temp, label, flag, source, k0, tc, ts):
    rows, cols, depth = temp.shape
    n = ngx * ngy
    block = lambda dtype: pltpu.VMEM((rows, cols, depth), dtype)
    padded = pltpu.VMEM((rows + 2, cols + 2 * PAD, depth), jnp.float32)
    f32 = jnp.float32
    out = jax.ShapeDtypeStruct((rows, cols, depth), f32)
    dma = pltpu.SemaphoreType.DMA
    return pl.pallas_call(
        functools.partial(kernel, ngx, ngy, cuts),
        out_shape=(out, out),
        in_specs=[pl.BlockSpec(memory_space=pl.ANY)] * 4
        + [pl.BlockSpec(memory_space=pltpu.SMEM)] * 3,
        out_specs=(pl.BlockSpec(memory_space=pltpu.VMEM),) * 2,
        scratch_shapes=[block(f32), block(jnp.int32), block(jnp.int32), block(f32)]
        + [padded] * 6
        + [pltpu.VMEM((rows + 1, cols, depth), f32)]
        + [block(f32)] * 6
        + [
            pltpu.VMEM((STEPS + 1, 16, depth), f32),
            pltpu.VMEM((STEPS + 1, 16, depth), f32),
            pltpu.VMEM((2, 8, 128), f32),
            pltpu.VMEM((2, n, 8, 128), f32),
            dma((4, 3)),
            dma((STEPS + 1, 2, cuts)),
            dma((STEPS + 1, 2, cuts)),
            dma((STEPS + 1, 2)),
            dma((STEPS + 1, 2)),
            dma((2, n)),
            dma((2, n)),
        ],
        compiler_params=pltpu.CompilerParams(
            collective_id=0, has_side_effects=True, vmem_limit_bytes=48 * 1024 * 1024
        ),
    )(temp, label, flag, source, k0, tc, ts)


def solution(mesh):
    block = P(("cycle", "gx"), "gy", None)
    shared = P("gx", "gy", None)
    return jax.shard_map(
        functools.partial(per_device, mesh.shape["gx"], mesh.shape["gy"], 2),
        mesh=mesh,
        in_specs=(block, shared, shared, block, P(), P(), P()),
        out_specs=(block, block),
        check_vma=False,
    )
```

time: 359 us -> 59.9 us (0.17)
  blocking collectives: 214 us -> 0 us
  other arithmetic: 58.6 us -> 0 us
  Pallas kernels: 0 us -> 51.4 us
  waiting for transfers between devices: 37.3 us -> 0 us
  starting transfers between devices: 33 us -> 0 us
  between operations: 10.1 us -> 0.65 us
    psum x7 -> x0, blocking collectives: 214 us -> none  [the longest x4 124 us: preconditioned_sum(): return lax.psum(jnp.sum(residual_now * pre_now), ('gx', 'gy'))]
    pallas_call x0 -> x1, Pallas kernels: none -> 51.4 us  [per_device(): pl.pallas_call(functools.partial(kernel, ngx, ngy, cuts), out_shape=(out,...]
    ppermute x20 -> x0, waiting for transfers between devices: 37.3 us -> none  [the longest x10 20.5 us: padded_2(): lax.ppermute(head, axis, [((i + 1) % count, i) for i in range(ends)])]
    ppermute x20 -> x0, starting transfers between devices: 33 us -> none  [the longest x10 20.1 us: padded_2(): lax.ppermute(tail, axis, [(i, (i + 1) % count) for i in range(ends)])]
    reduce_sum x7 -> x0, other arithmetic: 27 us -> none  [the longest x4 15.2 us: per_device(): alpha = norm_now / lax.psum(jnp.sum(direction * image), ('gx', 'gy'))]
    mul x1 -> x0, other arithmetic: 13.5 us -> none  [per_device(): substance_lookup(substance_label, zero_kelvin_diffusivity)]
    div x1 -> x0, other arithmetic: 7.91 us -> none  [per_device(): pre = residual / diag]
    unnamed x28 -> x14, local copies, waits for them, and re-layouts: 0.06 us -> 7.57 us
  transfers between devices with their start and end apart: 20 -> 0, of which waited for: 15 -> 0; matrix products, arithmetic and copies ran while one was open for 0% -> 0% of each run, Pallas kernels for 0% -> 0%
where the time goes in v1:
time: 59.9 us; the launch traced here: 59.6 us
  Pallas kernels  51.4 us (86%)
  local copies, waits for them, and re-layouts  7.57 us (13%)
  between operations  0.65 us (1%)
    pallas_call x1, Pallas kernels, per_device(): pl.pallas_call(functools.partial(kernel, ngx, ngy, cuts), out_shape=(out,...  51.4 us
    unnamed x14, local copies, waits for them, and re-layouts  7.57 us

profile of v1, /device:TPU:0, one launch (start us, length us, event | category | flops | bytes accessed | tf_op | source)
XLA Modules:
  0.0 59.6 jit_solution(7201108637001394108)
XLA Ops:
  0.6 0.0 copy-start
  0.6 1.2 %copy-done = f32[8,32,1024]{2,1,0:T(8,128)S(1)} copy-done((f32[8,32,1024]{2,1,0:T(8,128)S(1)}, f32[8,32,1024]{2,1,0:T(8,128)}, u32[]{:S(2)}) %copy-start) | copy-done | bytes 1048600
  1.9 0.0 copy-start.1
  1.9 1.2 %copy-done.1 = s32[8,32,1024]{2,1,0:T(8,128)S(1)} copy-done((s32[8,32,1024]{2,1,0:T(8,128)S(1)}, s32[8,32,1024]{2,1,0:T(8,128)}, u32[]{:S(2)}) %copy-start.1) | copy-done | bytes 1048600
  3.1 0.0 copy-start.2
  3.1 1.2 %copy-done.2 = s32[8,32,1024]{2,1,0:T(8,128)S(1)} copy-done((s32[8,32,1024]{2,1,0:T(8,128)S(1)}, s32[8,32,1024]{2,1,0:T(8,128)}, u32[]{:S(2)}) %copy-start.2) | copy-done | bytes 1048600
  4.3 0.0 copy-start.3
  4.3 0.7 %copy-done.3 = f32[8]{0:T(128)S(1)} copy-done((f32[8]{0:T(128)S(1)}, f32[8]{0:T(128)}, u32[]{:S(2)}) %copy-start.3) | copy-done | bytes 56
  5.0 0.0 copy-start.4
  5.0 0.7 %copy-done.4 = f32[8]{0:T(128)S(1)} copy-done((f32[8]{0:T(128)S(1)}, f32[8]{0:T(128)}, u32[]{:S(2)}) %copy-start.4) | copy-done | bytes 56
  5.6 0.0 copy-start.5
  5.6 0.7 %copy-done.5 = f32[8]{0:T(128)S(1)} copy-done((f32[8]{0:T(128)S(1)}, f32[8]{0:T(128)}, u32[]{:S(2)}) %copy-start.5) | copy-done | bytes 56
  6.3 51.4 %shard_map.86 = (f32[8,32,1024]{2,1,0:T(8,128)S(1)}, f32[8,32,1024]{2,1,0:T(8,128)S(1)}) custom-call(f32[8,32,1024]{2,1,0:T(8,128)S(1)} %copy-done, s32[8,32,1024]{2,1,0:T(8,128)S(1)} %copy-done.1, s32[8,32,1024]{2,1,0:T(8,128)S(1)} %copy-done.2, f32[8,32,1024]{2,1,0:T(8,128)} %source_hbm.1, f32[8]{0:T(128)S(1)} %copy-done.3, f32[8]{0:T(128)S(1)} %copy-done.4, ...), custom_call_target="tpu_custom_call" | custom-call | tf_op jit(solution)/shard_map/pallas_call | solution.py:486
  57.7 1.0 %copy.11 = f32[8,32,1024]{2,1,0:T(8,128)} copy(f32[8,32,1024]{2,1,0:T(8,128)S(1)} %get-tuple-element.4) | data formatting | bytes 2097152
  58.6 1.0 %copy.12 = f32[8,32,1024]{2,1,0:T(8,128)} copy(f32[8,32,1024]{2,1,0:T(8,128)S(1)} %get-tuple-element.5) | data formatting | bytes 2097152
Async XLA Ops:
  0.6 1.2 %copy-start = (f32[8,32,1024]{2,1,0:T(8,128)S(1)}, f32[8,32,1024]{2,1,0:T(8,128)}, u32[]{:S(2)}) copy-start(f32[8,32,1024]{2,1,0:T(8,128)} %temp_hbm.1) | copy-start | bytes 3145732
  1.9 1.2 %copy-start.1 = (s32[8,32,1024]{2,1,0:T(8,128)S(1)}, s32[8,32,1024]{2,1,0:T(8,128)}, u32[]{:S(2)}) copy-start(s32[8,32,1024]{2,1,0:T(8,128)} %label_hbm.1) | copy-start | bytes 3145732
  3.1 1.2 %copy-start.2 = (s32[8,32,1024]{2,1,0:T(8,128)S(1)}, s32[8,32,1024]{2,1,0:T(8,128)}, u32[]{:S(2)}) copy-start(s32[8,32,1024]{2,1,0:T(8,128)} %flag_hbm.1) | copy-start | bytes 3145732
  4.3 0.7 %copy-start.3 = (f32[8]{0:T(128)S(1)}, f32[8]{0:T(128)}, u32[]{:S(2)}) copy-start(f32[8]{0:T(128)} %k0_ref.1) | copy-start | bytes 100
  5.0 0.7 %copy-start.4 = (f32[8]{0:T(128)S(1)}, f32[8]{0:T(128)}, u32[]{:S(2)}) copy-start(f32[8]{0:T(128)} %tc_ref.1) | copy-start | bytes 100
  5.6 0.7 %copy-start.5 = (f32[8]{0:T(128)S(1)}, f32[8]{0:T(128)}, u32[]{:S(2)}) copy-start(f32[8]{0:T(128)} %ts_ref.1) | copy-start | bytes 100

commit v2 on v1

--- a/solution.py
+++ b/solution.py
@@ -30,20 +30,19 @@
 
 def kernel(
     ngx, ngy, cuts,
-    temp_hbm, label_hbm, flag_hbm, source_hbm, k0_ref, tc_ref, ts_ref,
+    temp_hbm, label_hbm, flag_hbm, source_hbm, k0_hbm, tc_hbm, ts_hbm,
     adjoint_ref, residual_ref,
-    temp, label, flag, source, cond, v0, v1, v2, v3, v4,
-    face_row, face_left, face_right, face_down, face_up, inv, diag,
+    k0_ref, tc_ref, ts_ref, temp, label, flag, source, fields,
+    scalars, sums, face_row, face_left, face_right, face_down, face_up, inv, diag,
     edge_out, edge_in, part_out, part_in,
-    load_sem, row_send, row_recv, edge_send, edge_recv, part_send, part_recv,
+    load_sem, table_sem, row_send, row_recv, edge_send, edge_recv, part_send, part_recv,
 ):
     rows, cols, depth = temp.shape
     tiles = cols // 8
     gx, gy = lax.axis_index("gx"), lax.axis_index("gy")
     n = ngx * ngy
     me = gx * ngy + gy
-    fields = (cond, v0, v1, v2, v3, v4)
-    v = fields[1:]
+    cond, v0 = fields.at[0], fields.at[1]
     has_lower, has_upper = gx > 0, gx < ngx - 1
 
     def peer(offset):
@@ -57,6 +56,12 @@
             src.at[pl.ds(first, size)], dst.at[pl.ds(first, size)], load_sem.at[a, group]
         )
 
+    tables = [
+        pltpu.make_async_copy(src, dst, table_sem.at[j])
+        for j, (src, dst) in enumerate(((k0_hbm, k0_ref), (tc_hbm, tc_ref), (ts_hbm, ts_ref)))
+    ]
+    for copy in tables:
+        copy.start()
     order = [(a, g) for a in (0, 1) for g in (0, 1)] + [(a, g) for a in (2, 3) for g in (0, 1)]
     order += [(a, 2) for a in range(4)]
     for a, g in order:
@@ -73,42 +78,46 @@
     zero_row = jnp.zeros((cols, depth), jnp.float32)
     zero_edge = jnp.zeros((8, depth), jnp.float32)
 
-    @pl.when(jnp.logical_not(has_lower))
-    def _():
-        for field in fields[:-1]:
-            field[0, PAD : PAD + cols, :] = zero_row
-
-    @pl.when(jnp.logical_not(has_upper))
-    def _():
-        for field in fields[:-1]:
-            field[rows + 1, PAD : PAD + cols, :] = zero_row
-
-    for field in fields[:-1]:
-        for i in range(1, rows + 1):
-            field[i, 0:PAD, :] = zero_edge
-            field[i, PAD + cols : PAD + cols + 8, :] = zero_edge
-    for k in range(STEPS + 1):
+    def clear(k, carry):
+        @pl.when(jnp.logical_not(has_lower))
+        def _():
+            fields[k, 0, PAD : PAD + cols, :] = zero_row
+
+        @pl.when(jnp.logical_not(has_upper))
+        def _():
+            fields[k, rows + 1, PAD : PAD + cols, :] = zero_row
+
+        def clear_edge(i, carry):
+            fields[k, i, 0:PAD, :] = zero_edge
+            fields[k, i, PAD + cols : PAD + cols + 8, :] = zero_edge
+            return carry
+
+        lax.fori_loop(1, rows + 1, clear_edge, 0)
         edge_out[k, 0:8, :] = zero_edge
         edge_out[k, 8:16, :] = zero_edge
+        return carry
+
+    lax.fori_loop(0, STEPS + 1, clear, 0)
 
     width = cols // cuts
     own_edge = jnp.where(gy == 0, PAD + cols - 1, PAD)
     halo_edge = jnp.where(gy == 0, PAD + cols, PAD - 1)
 
     def row_copy(k, side, c):
-        src, dst = ((1, rows + 1), (rows, 0))[side]
+        src = 1 + side * (rows - 1)
+        dst = (1 - side) * (rows + 1)
         part = pl.ds(PAD + c * width, width)
         return pltpu.make_async_remote_copy(
-            src_ref=fields[k].at[src, part, :],
-            dst_ref=fields[k].at[dst, part, :],
+            src_ref=fields.at[k, src, part, :],
+            dst_ref=fields.at[k, dst, part, :],
             send_sem=row_send.at[k, side, c],
             recv_sem=row_recv.at[k, side, c],
-            device_id={"gx": gx - 1 if side == 0 else gx + 1},
+            device_id={"gx": gx - 1 + 2 * side},
             device_id_type=MESH,
         )
 
     def has(side):
-        return has_lower if side == 0 else has_upper
+        return jnp.where(side == 0, gx, ngx - 1 - gx) > 0
 
     def send_row(k, side, c):
         @pl.when(has(side))
@@ -131,17 +140,35 @@
             device_id_type=MESH,
         )
 
-    spots = ([(1, 0), (rows, 1)], [(i, 8 + i - 2) for i in range(2, rows)])
+    def outer(j):
+        return 1 + j * (rows - 1), j
+
+    def others(j):
+        return j + 2, j + 8
+
+    groups = ((2, outer), (rows - 2, others))
 
     def send_edge(k, group):
-        for i, spot in spots[group]:
-            edge_out[k, spot : spot + 1, :] = fields[k][i, pl.ds(own_edge, 1), :]
+        count, spot_of = groups[group]
+
+        def one(j, carry):
+            i, spot = spot_of(j)
+            edge_out[k, pl.ds(spot, 1), :] = fields[k, i, pl.ds(own_edge, 1), :]
+            return carry
+
+        lax.fori_loop(0, count, one, 0)
         edge_copy(k, group).start()
 
     def wait_edge(k, group):
         edge_copy(k, group).wait_recv()
-        for i, spot in spots[group]:
-            fields[k][i, pl.ds(halo_edge, 1), :] = edge_in[k, spot : spot + 1, :]
+        count, spot_of = groups[group]
+
+        def one(j, carry):
+            i, spot = spot_of(j)
+            fields[k, i, pl.ds(halo_edge, 1), :] = edge_in[k, pl.ds(spot, 1), :]
+            return carry
+
+        lax.fori_loop(0, count, one, 0)
 
     def table(ref, marks):
         out = jnp.zeros(marks[0].shape, jnp.float32)
@@ -157,7 +184,7 @@
             1.0 + table(tc_ref, marks) * temp[i - 1, part, :]
         )
 
-    def start_row(i, t, end):
+    def start_row(i, t):
         at = PAD + 8 * t
         part = pl.ds(8 * t, 8)
         c = cond[i, pl.ds(at, 8), :]
@@ -189,7 +216,7 @@
     def apply(k, i, t):
         at = PAD + 8 * t
         part = pl.ds(8 * t, 8)
-        field = v[k]
+        field = fields.at[k + 1]
         x = field[i, pl.ds(at, 8), :]
         w = face_row[i - 1, part, :] * field[i - 1, pl.ds(at, 8), :]
         w += face_row[i, part, :] * field[i + 1, pl.ds(at, 8), :]
@@ -198,7 +225,7 @@
         w += face_down[i - 1, part, :] * pltpu.roll(x, 1, 1)
         w += face_up[i - 1, part, :] * pltpu.roll(x, depth - 1, 1)
         y = w * inv[i - 1, part, :]
-        v[k + 1][i, pl.ds(at, 8), :] = y
+        fields[k + 2, i, pl.ds(at, 8), :] = y
         return w, x, y
 
     zero = jnp.zeros((8, 128), jnp.float32)
@@ -214,9 +241,9 @@
             device_id_type=MESH,
         )
 
-    def send_parts(which, sums):
+    def send_parts(which, terms):
         tile = zero
-        for d, s in enumerate(sums):
+        for d, s in enumerate(terms):
             tile = jnp.where(lane128 == d, jnp.sum(s, axis=(0, 1), keepdims=True), tile)
         part_out[which] = tile
 
@@ -249,27 +276,31 @@
     def tiles_of(c):
         return range(c * width // 8, (c + 1) * width // 8)
 
-    ends = ((0, 1), (1, rows))
-
+    def each_end(visit, carry):
+        def one(end, carry):
+            return visit(end, 1 + end * (rows - 1), carry)
+
+        return lax.fori_loop(0, 2, one, carry)
+
+    for copy in tables:
+        copy.wait()
     for a in (0, 1):
         for g in (0, 1):
             load(a, g).wait()
-    for end, i in ends:
+
+    def conduct_row(i, carry):
         for t in range(tiles):
             conduct(i, t)
+        return carry
+
+    each_end(lambda end, i, carry: conduct_row(i, carry), 0)
     pl.semaphore_wait(barrier, n - 1)
     for c in range(cuts):
-        for end, i in ends:
+        for end in (0, 1):
             send_row(0, end, c)
     send_edge(0, 0)
     load(0, 2).wait()
     load(1, 2).wait()
-
-    def conduct_row(i, carry):
-        for t in range(tiles):
-            conduct(i, t)
-        return carry
-
     lax.fori_loop(2, rows, conduct_row, 0)
     send_edge(0, 1)
 
@@ -277,13 +308,17 @@
         for g in (0, 1):
             load(a, g).wait()
     wait_edge(0, 0)
-    sums = [zero]
+    acc = zero
     for c in range(cuts):
-        for end, i in ends:
+
+        def start_end(end, i, acc, c=c):
             wait_row(0, end, c)
             for t in tiles_of(c):
-                sums[0] = sums[0] + start_row(i, t, end)
+                acc = acc + start_row(i, t)
             send_row(1, end, c)
+            return acc
+
+        acc = each_end(start_end, acc)
     send_edge(1, 0)
     load(2, 2).wait()
     load(3, 2).wait()
@@ -291,48 +326,65 @@
 
     def start_rows(i, acc):
         for t in range(tiles):
-            acc = acc + start_row(i, t, None)
+            acc = acc + start_row(i, t)
         return acc
 
-    sums[0] = lax.fori_loop(2, rows, start_rows, sums[0])
+    sums[0] = lax.fori_loop(2, rows, start_rows, acc)
     send_edge(1, 1)
 
-    theta = bend = shift = gain = None
-    for k in range(STEPS):
-        last = k == STEPS - 1
-
-        def visit(i, t, acc, k=k):
+    def step(k, carry):
+        more = k < STEPS - 1
+
+        def visit(i, t, acc):
             w, x, y = apply(k, i, t)
-            if k < 2:
-                return (acc[0] + fold(w * x), acc[1] + fold(w * y))
-            return acc
+            if k >= 2:
+                return acc
+            return (acc[0] + fold(w * x), acc[1] + fold(w * y))
 
         acc = (zero, zero)
         wait_edge(k + 1, 0)
         for c in range(cuts):
-            for end, i in ends:
+
+            def visit_end(end, i, acc, c=c):
                 wait_row(k + 1, end, c)
                 for t in tiles_of(c):
                     acc = visit(i, t, acc)
-                if not last:
+
+                @pl.when(more)
+                def _():
                     send_row(k + 2, end, c)
-        if not last:
+
+                return acc
+
+            acc = each_end(visit_end, acc)
+
+        @pl.when(more)
+        def _():
             send_edge(k + 2, 0)
+
         wait_edge(k + 1, 1)
 
-        def visit_row(i, acc, visit=visit):
+        def visit_row(i, acc):
             for t in range(tiles):
                 acc = visit(i, t, acc)
             return acc
 
         acc = lax.fori_loop(2, rows, visit_row, acc)
-        if not last:
+
+        @pl.when(more)
+        def _():
             send_edge(k + 2, 1)
+
         if k < 2:
-            sums += list(acc)
-        if k == 1:
-            send_parts(0, sums)
-        if k == 2:
+            sums[2 * k + 1] = acc[0]
+            sums[2 * k + 2] = acc[1]
+
+        @pl.when(k == 1)
+        def _():
+            send_parts(0, [sums[j] for j in range(5)])
+
+        @pl.when(k == 2)
+        def _():
             m = take_parts(0, 5)
             theta = m[1] / m[0]
             size = m[2] - theta * m[1]
@@ -340,8 +392,17 @@
             turn = m[3] - 2.0 * theta * m[2] + theta * theta * m[1]
             shift = jnp.where(size > 0.0, turn / jnp.where(size > 0.0, size, 1.0), 0.0)
             shift = jnp.minimum(jnp.maximum(shift, -1.0), 1.0)
-            bend = shift * theta - gain
-            slope = -(shift + theta)
+            scalars[0] = theta
+            scalars[1] = shift
+            scalars[2] = gain
+
+        return carry
+
+    for k in range(STEPS):
+        step(k, 0)
+    theta, shift, gain = scalars[0], scalars[1], scalars[2]
+    slope = -(shift + theta)
+    bend = shift * theta - gain
 
     wide = lambda x: x[:, 0:1] * jnp.ones((1, depth), jnp.float32)
     theta_w, slope_w, bend_w = wide(theta), wide(slope), wide(bend)
@@ -351,7 +412,7 @@
         acc = list(acc)
         for t in range(tiles):
             at = pl.ds(PAD + 8 * t, 8)
-            f = [u[i, at, :] for u in v]
+            f = [fields[j, i, at, :] for j in range(1, STEPS + 2)]
             d = diag[i - 1, pl.ds(8 * t, 8), :]
             q = [
                 f[0],
@@ -445,7 +506,7 @@
         for t in range(tiles):
             at = pl.ds(PAD + 8 * t, 8)
             part = pl.ds(8 * t, 8)
-            f = [u[i, at, :] for u in v]
+            f = [fields[j, i, at, :] for j in range(1, STEPS + 2)]
             x = adj_w[0] * f[0]
             for j in range(1, 4):
                 x += adj_w[j] * f[j]
@@ -458,14 +519,21 @@
 
     lax.fori_loop(1, rows + 1, finish_row, 0)
 
-    for k in range(STEPS + 1):
+    def left(k, carry):
         for group in (0, 1):
             edge_copy(k, group).wait_send()
-        for side in (0, 1):
+
+        def one(side, carry):
             @pl.when(has(side))
-            def _(k=k, side=side):
+            def _():
                 for c in range(cuts):
                     row_copy(k, side, c).wait_send()
+
+            return carry
+
+        return lax.fori_loop(0, 2, one, carry)
+
+    lax.fori_loop(0, STEPS + 1, left, 0)
 
     def sent(offset, carry):
         for which in (0, 1):
@@ -479,18 +547,18 @@
     rows, cols, depth = temp.shape
     n = ngx * ngy
     block = lambda dtype: pltpu.VMEM((rows, cols, depth), dtype)
-    padded = pltpu.VMEM((rows + 2, cols + 2 * PAD, depth), jnp.float32)
+    padded = pltpu.VMEM((STEPS + 2, rows + 2, cols + 2 * PAD, depth), jnp.float32)
     f32 = jnp.float32
     out = jax.ShapeDtypeStruct((rows, cols, depth), f32)
     dma = pltpu.SemaphoreType.DMA
     return pl.pallas_call(
         functools.partial(kernel, ngx, ngy, cuts),
         out_shape=(out, out),
-        in_specs=[pl.BlockSpec(memory_space=pl.ANY)] * 4
-        + [pl.BlockSpec(memory_space=pltpu.SMEM)] * 3,
+        in_specs=[pl.BlockSpec(memory_space=pltpu.HBM)] * 7,
         out_specs=(pl.BlockSpec(memory_space=pltpu.VMEM),) * 2,
-        scratch_shapes=[block(f32), block(jnp.int32), block(jnp.int32), block(f32)]
-        + [padded] * 6
+        scratch_shapes=[pltpu.SMEM(k0.shape, f32)] * 3
+        + [block(f32), block(jnp.int32), block(jnp.int32), block(f32)]
+        + [padded, pltpu.VMEM((3, 8, 128), f32), pltpu.VMEM((5, 8, 128), f32)]
         + [pltpu.VMEM((rows + 1, cols, depth), f32)]
         + [block(f32)] * 6
         + [
@@ -499,6 +567,7 @@
             pltpu.VMEM((2, 8, 128), f32),
             pltpu.VMEM((2, n, 8, 128), f32),
             dma((4, 3)),
+            dma((3,)),
             dma((STEPS + 1, 2, cuts)),
             dma((STEPS + 1, 2, cuts)),
             dma((STEPS + 1, 2)),
@@ -507,7 +576,7 @@
             dma((2, n)),
         ],
         compiler_params=pltpu.CompilerParams(
-            collective_id=0, has_side_effects=True, vmem_limit_bytes=48 * 1024 * 1024
+            collective_id=0, has_side_effects=True, vmem_limit_bytes=62 * 1024 * 1024
         ),
     )(temp, label, flag, source, k0, tc, ts)
 
@@ -516,7 +585,7 @@
     block = P(("cycle", "gx"), "gy", None)
     shared = P("gx", "gy", None)
     return jax.shard_map(
-        functools.partial(per_device, mesh.shape["gx"], mesh.shape["gy"], 2),
+        functools.partial(per_device, mesh.shape["gx"], mesh.shape["gy"], 4),
         mesh=mesh,
         in_specs=(block, shared, shared, block, P(), P(), P()),
         out_specs=(block, block),

time: 59.9 us -> 53.5 us (0.89)
  local copies, waits for them, and re-layouts: 7.57 us -> 3.37 us
  Pallas kernels: 51.4 us -> 49.3 us
    unnamed x14 -> x4, local copies, waits for them, and re-layouts: 7.57 us -> 3.37 us
    pallas_call x1, Pallas kernels: 51.4 us -> 49.3 us  [per_device(): pl.pallas_call(functools.partial(kernel, ngx, ngy, cuts), out_shape=(out,...]
where the time goes in v2:
time: 53.5 us; the launch traced here: 53.3 us
  Pallas kernels  49.3 us (92%)
  local copies, waits for them, and re-layouts  3.37 us (6%)
  between operations  0.65 us (1%)
    pallas_call x1, Pallas kernels, per_device(): pl.pallas_call(functools.partial(kernel, ngx, ngy, cuts), out_shape=(out,...  49.3 us
    unnamed x4, local copies, waits for them, and re-layouts  3.37 us

profile of v2, /device:TPU:0, one launch (start us, length us, event | category | flops | bytes accessed | tf_op | source)
XLA Modules:
  0.0 53.3 jit_solution(5878018497274381851)
XLA Ops:
  0.6 49.3 %shard_map.86 = (f32[8,32,1024]{2,1,0:T(8,128)}, f32[8,32,1024]{2,1,0:T(8,128)}) custom-call(f32[8,32,1024]{2,1,0:T(8,128)} %temp_hbm.1, s32[8,32,1024]{2,1,0:T(8,128)} %label_hbm.1, s32[8,32,1024]{2,1,0:T(8,128)} %flag_hbm.1, f32[8,32,1024]{2,1,0:T(8,128)} %source_hbm.1, f32[8]{0:T(128)} %k0_hbm.1, f32[8]{0:T(128)} %tc_hbm.1, f32[8]{0:T(128)} %ts_hbm.1), custom_call_target="tpu_custom_call" | custom-call | tf_op jit(solution)/shard_map/pallas_call | solution.py:554
  50.0 0.0 copy-start
  50.0 2.4 %copy.11 = f32[8,32,1024]{2,1,0:T(8,128)} copy(f32[8,32,1024]{2,1,0:T(8,128)} %get-tuple-element.4) | data formatting | bytes 2097152
  52.4 0.0 copy-done
  52.4 1.0 %copy.12 = f32[8,32,1024]{2,1,0:T(8,128)} copy(f32[8,32,1024]{2,1,0:T(8,128)S(1)} %copy-done) | data formatting | bytes 2097152
Async XLA Ops:
  50.0 2.4 %copy-start = (f32[8,32,1024]{2,1,0:T(8,128)S(1)}, f32[8,32,1024]{2,1,0:T(8,128)}, u32[]{:S(2)}) copy-start(f32[8,32,1024]{2,1,0:T(8,128)} %get-tuple-element.5) | copy-start | bytes 3145732

commit v3 on v2

--- a/solution.py
+++ b/solution.py
@@ -332,6 +332,41 @@
     sums[0] = lax.fori_loop(2, rows, start_rows, acc)
     send_edge(1, 1)
 
+    wide = lambda x: x[:, 0:1] * jnp.ones((1, depth), jnp.float32)
+    early = [(a, b) for a in range(4) for b in range(a, 4)]
+    late = [(a, 4) for a in range(4)]
+    pairs = early + late
+
+    def gram_of(first):
+        theta, shift, gain = scalars[0], scalars[1], scalars[2]
+        theta_w = wide(theta)
+        slope_w = wide(-(shift + theta))
+        bend_w = wide(shift * theta - gain)
+        here = early if first else late
+
+        def gram_row(i, acc):
+            acc = list(acc)
+            for t in range(tiles):
+                at = pl.ds(PAD + 8 * t, 8)
+                f = [fields[j, i, at, :] for j in range(1, STEPS + (1 if first else 2))]
+                d = diag[i - 1, pl.ds(8 * t, 8), :]
+                q = [f[0], f[1] - theta_w * f[0]]
+                for j in range(2, len(f)):
+                    q.append(f[j] + slope_w * f[j - 1] + bend_w * f[j - 2])
+                if first:
+                    for a in range(4):
+                        dq = d * q[a]
+                        for b in range(a, 4):
+                            spot = here.index((a, b))
+                            acc[spot] = acc[spot] + fold(dq * q[b])
+                else:
+                    dq = d * q[4]
+                    for a in range(4):
+                        acc[a] = acc[a] + fold(dq * q[a])
+            return tuple(acc)
+
+        return lax.fori_loop(1, rows + 1, gram_row, (zero,) * len(here))
+
     def step(k, carry):
         more = k < STEPS - 1
 
@@ -395,6 +430,8 @@
             scalars[0] = theta
             scalars[1] = shift
             scalars[2] = gain
+            for j, value in enumerate(gram_of(True)):
+                sums[5 + j] = value
 
         return carry
 
@@ -404,31 +441,8 @@
     slope = -(shift + theta)
     bend = shift * theta - gain
 
-    wide = lambda x: x[:, 0:1] * jnp.ones((1, depth), jnp.float32)
-    theta_w, slope_w, bend_w = wide(theta), wide(slope), wide(bend)
-    pairs = [(a, b) for a in range(4) for b in range(a, 5)]
-
-    def gram_row(i, acc):
-        acc = list(acc)
-        for t in range(tiles):
-            at = pl.ds(PAD + 8 * t, 8)
-            f = [fields[j, i, at, :] for j in range(1, STEPS + 2)]
-            d = diag[i - 1, pl.ds(8 * t, 8), :]
-            q = [
-                f[0],
-                f[1] - theta_w * f[0],
-                f[2] + slope_w * f[1] + bend_w * f[0],
-                f[3] + slope_w * f[2] + bend_w * f[1],
-                f[4] + slope_w * f[3] + bend_w * f[2],
-            ]
-            for a in range(4):
-                dq = d * q[a]
-                for b in range(a, 5):
-                    spot = pairs.index((a, b))
-                    acc[spot] = acc[spot] + fold(dq * q[b])
-        return tuple(acc)
-
-    grams = lax.fori_loop(1, rows + 1, gram_row, (zero,) * len(pairs))
+    grams = gram_of(False)
+    grams = [sums[5 + j] for j in range(len(early))] + list(grams)
     send_parts(1, grams)
     m = take_parts(1, len(pairs))
     gram = {}
@@ -558,7 +572,7 @@
         out_specs=(pl.BlockSpec(memory_space=pltpu.VMEM),) * 2,
         scratch_shapes=[pltpu.SMEM(k0.shape, f32)] * 3
         + [block(f32), block(jnp.int32), block(jnp.int32), block(f32)]
-        + [padded, pltpu.VMEM((3, 8, 128), f32), pltpu.VMEM((5, 8, 128), f32)]
+        + [padded, pltpu.VMEM((3, 8, 128), f32), pltpu.VMEM((15, 8, 128), f32)]
         + [pltpu.VMEM((rows + 1, cols, depth), f32)]
         + [block(f32)] * 6
         + [

time: 53.5 us -> 52.9 us (0.989)
  Pallas kernels: 49.3 us -> 48.7 us
    pallas_call x1, Pallas kernels: 49.3 us -> 48.7 us  [per_device(): pl.pallas_call(functools.partial(kernel, ngx, ngy, cuts), out_shape=(out,...]
where the time goes in v3:
time: 52.9 us; the launch traced here: 52.7 us
  Pallas kernels  48.7 us (92%)
  local copies, waits for them, and re-layouts  3.37 us (6%)
  between operations  0.65 us (1%)
    pallas_call x1, Pallas kernels, per_device(): pl.pallas_call(functools.partial(kernel, ngx, ngy, cuts), out_shape=(out,...  48.7 us
    unnamed x4, local copies, waits for them, and re-layouts  3.37 us

profile of v3, /device:TPU:0, one launch (start us, length us, event | category | flops | bytes accessed | tf_op | source)
XLA Modules:
  0.0 52.7 jit_solution(15551817701635045890)
XLA Ops:
  0.6 48.7 %shard_map.86 = (f32[8,32,1024]{2,1,0:T(8,128)}, f32[8,32,1024]{2,1,0:T(8,128)}) custom-call(f32[8,32,1024]{2,1,0:T(8,128)} %temp_hbm.1, s32[8,32,1024]{2,1,0:T(8,128)} %label_hbm.1, s32[8,32,1024]{2,1,0:T(8,128)} %flag_hbm.1, f32[8,32,1024]{2,1,0:T(8,128)} %source_hbm.1, f32[8]{0:T(128)} %k0_hbm.1, f32[8]{0:T(128)} %tc_hbm.1, f32[8]{0:T(128)} %ts_hbm.1), custom_call_target="tpu_custom_call" | custom-call | tf_op jit(solution)/shard_map/pallas_call | solution.py:568
  49.3 0.0 copy-start
  49.4 2.4 %copy.11 = f32[8,32,1024]{2,1,0:T(8,128)} copy(f32[8,32,1024]{2,1,0:T(8,128)} %get-tuple-element.4) | data formatting | bytes 2097152
  51.8 0.0 copy-done
  51.8 1.0 %copy.12 = f32[8,32,1024]{2,1,0:T(8,128)} copy(f32[8,32,1024]{2,1,0:T(8,128)S(1)} %copy-done) | data formatting | bytes 2097152
Async XLA Ops:
  49.3 2.4 %copy-start = (f32[8,32,1024]{2,1,0:T(8,128)S(1)}, f32[8,32,1024]{2,1,0:T(8,128)}, u32[]{:S(2)}) copy-start(f32[8,32,1024]{2,1,0:T(8,128)} %get-tuple-element.5) | copy-start | bytes 3145732
